TPU v7x, 32 devices: a whole 2x2x4 slice. The times are simulated.
32 devices in a mesh: slab: 8 (over z, y), cross: 4 (over x, core).
Axes of the slice: x: 2, y: 2, z: 4, core: 2. Of those that a mesh axis runs over, the one named last changes fastest.
Arguments:
- state: float32 [5, 16, 4096], P(None, 'slab', 'cross'), may hold values from -1.2 to 1.2
- rhs: float32 [5, 16, 4096], P(None, 'slab', 'cross'), may hold values from -1.2 to 1.2
- dinv: float32 [5, 5, 16, 4096], P(None, None, 'slab', 'cross'), may hold values from -0.3 to 2.3, as said below
- lower_jac: float32 [5, 5, 16, 4096], P(None, None, 'slab', 'cross'), may hold values from -0.3 to 2.3
- upper_jac: float32 [5, 5, 16, 4096], P(None, None, 'slab', 'cross'), may hold values from -0.3 to 2.3
- owner: int32 [32768, 1], P(('slab', 'cross')), may hold values from 0 to 31; in each aligned block of 1024 rows (0 to 1023, 1024 to 2047, ...) at most 128 rows name the same one
- donor_block: int32 [32768], P(('slab', 'cross')), may hold values from 0 to 15
- offsets: int32 [8, 32768], P(None, ('slab', 'cross')), may hold values from 0 to 127
- weights: float32 [8, 32768], P(None, ('slab', 'cross')), may hold values from 0 to 1, as said below
- receptor_perm: int32 [32, 16], P(('slab', 'cross')), may hold values from 0 to 15, each once within a row
Outputs:
- update: float32 [5, 16, 4096], P(None, 'slab', 'cross')
Inputs may be any that keep to these rules, and one draw needn't show every extreme that they name: `dinv`: each is s (I + E) with s between 0.5 and 2 a cell and small E. `weights`: positive; the 8 weights of one fringe point sum to one. Among the 1024 fringe points of one device no owner is named more than 128 times.
All inputs are finite; a program needn't handle non-finite values.
Results may differ from a plain program's by a relative error of at most 0.00021.
Values sent between devices are 32-bit elements; how exact they have to be, the bound alone decides.
A program may use at most 64 MiB of HBM per device.

v0:
```python
import jax
import jax.numpy as jnp
from jax import lax
from jax.sharding import PartitionSpec as P

BLOCK_CELLS = 128


def from_behind(array, axis, by):
    peers = lax.axis_size(axis)
    pairs = [(i, i + by) for i in range(peers) if 0 <= i + by < peers]
    return lax.ppermute(array, axis, pairs)


def apply_block(matrix, vector):
    return jnp.sum(matrix * vector[None], axis=1)


def chain_blocks(later, earlier):
    return jnp.sum(later[:, :, None] * earlier[None], axis=1)


def plane_of(array, index):
    return lax.dynamic_index_in_dim(array, index, axis=array.ndim - 2, keepdims=False)


def unit_blocks(width, cells):
    return jnp.broadcast_to(jnp.eye(width, dtype=jnp.float32)[:, :, None], (width, width, cells))


def lower_digest_state(dinv, lower_jac, forcing):
    width, planes, cells = forcing.shape

    def step(carry, index):
        transfer, value = carry
        inverse = plane_of(dinv, index)
        coupling = plane_of(lower_jac, index)
        value = apply_block(inverse, plane_of(forcing, index) + apply_block(coupling, value))
        transfer = chain_blocks(chain_blocks(inverse, coupling), transfer)
        return ((transfer, value), None)

    start = (unit_blocks(width, cells), jnp.zeros((width, cells), jnp.float32))
    result, _ = lax.scan(step, start, jnp.arange(planes))
    return result


def lower_sweep(dinv, lower_jac, forcing, entry):
    planes = forcing.shape[1]

    def step(value, index):
        inverse = plane_of(dinv, index)
        value = apply_block(
            inverse, plane_of(forcing, index) + apply_block(plane_of(lower_jac, index), value)
        )
        return (value, value)

    _, stacked = lax.scan(step, entry, jnp.arange(planes))
    return stacked


def upper_summary(dinv, upper_jac, lower_planes):
    planes, width, cells = lower_planes.shape

    def step(carry, index):
        transfer, value = carry
        inverse = plane_of(dinv, index)
        coupling = plane_of(upper_jac, index)
        partial_value = lax.dynamic_index_in_dim(lower_planes, index, axis=0, keepdims=False)
        value = partial_value + apply_block(inverse, apply_block(coupling, value))
        transfer = chain_blocks(chain_blocks(inverse, coupling), transfer)
        return ((transfer, value), None)

    start = (unit_blocks(width, cells), jnp.zeros((width, cells), jnp.float32))
    result, _ = lax.scan(step, start, jnp.arange(planes), reverse=True)
    return result


def upper_sweep(dinv, upper_jac, lower_planes, entry):
    planes = lower_planes.shape[0]

    def step(value, index):
        inverse = plane_of(dinv, index)
        partial_value = lax.dynamic_index_in_dim(lower_planes, index, axis=0, keepdims=False)
        value = partial_value + apply_block(inverse, apply_block(plane_of(upper_jac, index), value))
        return (value, value)

    _, stacked = lax.scan(step, entry, jnp.arange(planes), reverse=True)
    return stacked


def body(
    state, rhs, dinv, lower_jac, upper_jac, owner, donor_block, offsets, weights, receptor_perm
):
    width, planes, cells = state.shape
    resident_cells = planes * cells
    state_flat = state.reshape(width, resident_cells)
    devices = lax.axis_size(("slab", "cross"))
    fringe_rows = owner.shape[0]
    capacity = 4 * fringe_rows // devices
    corners = offsets.shape[0]
    target = owner[:, 0]
    onehot = (target[:, None] == jnp.arange(devices, dtype=jnp.int32)[None, :]).astype(jnp.int32)
    slot = jnp.sum(jnp.cumsum(onehot, axis=0) * onehot, axis=1) - 1
    flat_slot = target * capacity + slot
    wanted = donor_block[None, :] * BLOCK_CELLS + offsets
    request = jnp.zeros((corners, devices * capacity), jnp.int32).at[:, flat_slot].set(wanted)
    request = request.reshape(corners, devices, capacity)
    found = state_flat[
        :, lax.all_to_all(request, ("slab", "cross"), split_axis=1, concat_axis=1, tiled=True)
    ]
    arrived = lax.all_to_all(found, ("slab", "cross"), split_axis=2, concat_axis=2, tiled=True)
    picked = arrived[:, :, target, slot]
    interp = jnp.sum(weights[None] * picked, axis=1)
    fringe_blocks = fringe_rows // BLOCK_CELLS
    chosen = receptor_perm[0, :fringe_blocks]
    targets = (
        chosen[:, None] * BLOCK_CELLS + jnp.arange(BLOCK_CELLS, dtype=jnp.int32)[None, :]
    ).reshape(fringe_rows)
    forcing = rhs.reshape(width, resident_cells).at[:, targets].set(interp - state_flat[:, targets])
    forcing = forcing.reshape(width, planes, cells)
    lower_mapping, low_last = lower_digest_state(dinv, lower_jac, forcing)
    empty = jnp.zeros((width, cells), jnp.float32)
    turns = lax.axis_size("slab") - 1

    def lower_turn(count, carry):
        held, arriving = carry
        arriving = from_behind(held, "slab", 1)
        return (apply_block(lower_mapping, arriving) + low_last, arriving)

    _, low_entry = lax.fori_loop(0, turns, lower_turn, (low_last, empty))
    lower_planes = lower_sweep(dinv, lower_jac, forcing, low_entry)
    ascending_table, up_first = upper_summary(dinv, upper_jac, lower_planes)

    def upper_turn(count, carry):
        held, arriving = carry
        arriving = from_behind(held, "slab", -1)
        return (apply_block(ascending_table, arriving) + up_first, arriving)

    _, up_entry = lax.fori_loop(0, turns, upper_turn, (up_first, empty))
    result = upper_sweep(dinv, upper_jac, lower_planes, up_entry)
    return jnp.moveaxis(result, 0, 1)


def solution(mesh):
    return jax.shard_map(
        body,
        mesh=mesh,
        in_specs=(
            P(None, "slab", "cross"),
            P(None, "slab", "cross"),
            P(None, None, "slab", "cross"),
            P(None, None, "slab", "cross"),
            P(None, None, "slab", "cross"),
            P(("slab", "cross"), None),
            P(("slab", "cross")),
            P(None, ("slab", "cross")),
            P(None, ("slab", "cross")),
            P(("slab", "cross"), None),
        ),
        out_specs=P(None, "slab", "cross"),
        check_vma=False,
    )
```

profile of v0, /device:TPU:0, one launch (start us, length us, event | category | flops | bytes accessed | tf_op | source)
XLA Modules:
  0.0 343.7 jit_solution(15856560875654733394)
XLA Ops:
  0.7 9.0 %reduce-window.6 = s32[32,8,128]{2,1,0:T(8,128)S(1)} reduce-window(s32[32,8,128]{2,1,0:T(8,128)S(1)} %fusion.11, s32[]{:T(128)} %constant.168.clone.1), window={size=1x1x128 pad=0_0x0_0x127_0}, to_apply=%region_0.0 | reduce-window | flops 4161536 | bytes 262148 | tf_op jit(solution)/shard_map/reduce-window
  13.3 3.6 %scatter_custom_fusion = s32[8,4096]{0,1:T(8,128)S(1)} fusion(s32[1024]{0:T(1024)S(1)} %bitcast.149, s32[1024,8]{1,0:T(8,128)S(1)} %copy.48, s32[]{:T(128)} %constant.168.clone.1), kind=kCustom, calls=%fused_computation.42 | custom fusion | bytes 131076 | tf_op jit(solution)/shard_map/scatter | solution.py:106
  18.1 7.3 %all-to-all-start = ((s32[8,32,128]{2,0,1:T(8,128)}), s32[8,32,128]{2,0,1:T(8,128)S(1)}, u32[]{:S(2)}, u32[]{:S(2)}) async-start(s32[8,32,128]{2,0,1:T(8,128)} %copy.49), calls=%async_computation | async-start | bytes 262144 | tf_op jit(solution)/shard_map/all_to_all | solution.py:109
  25.8 7.9 %all-to-all-done = s32[8,32,128]{2,0,1:T(8,128)S(1)} async-done(((s32[8,32,128]{2,0,1:T(8,128)}), s32[8,32,128]{2,0,1:T(8,128)S(1)}, u32[]{:S(2)}, u32[]{:S(2)}) %all-to-all-start) | async-done | bytes 131104 | tf_op jit(solution)/shard_map/all_to_all | solution.py:109
  33.7 108.2 %gather_fusion = f32[32768,5]{1,0:T(8,128)} fusion(f32[5,2048]{0,1:T(8,128)S(1)} %bitcast.131, s32[32768]{0:T(1024)S(1)} %broadcast_clamp_fusion), kind=kCustom, calls=%fused_computation | custom fusion | bytes 1441792 | tf_op jit(solution)/shard_map/gather | solution.py:108
  141.9 10.5 %copy.53 = f32[8,32,128,5]{2,0,3,1:T(8,128)} copy(f32[8,32,128,5]{3,2,1,0:T(8,128)} %bitcast.133) | data formatting | bytes 1310720 | tf_op jit(solution)/shard_map/gather | solution.py:108
  152.4 3.3 all-to-all-start.1
  157.4 16.3 %all-to-all-done.1 = f32[5,8,32,128]{3,1,0,2:T(8,128)} async-done(((f32[5,8,32,128]{3,1,0,2:T(8,128)}), f32[5,8,32,128]{3,1,0,2:T(8,128)}, u32[]{:S(2)}, u32[]{:S(2)}) %all-to-all-start.1) | async-done | bytes 655392 | tf_op jit(solution)/shard_map/all_to_all | solution.py:111
  173.7 9.4 %copy.54 = f32[5,8,32,128]{1,0,3,2:T(8,128)} copy(f32[5,8,32,128]{3,1,0,2:T(8,128)} %all-to-all-done.1) | data formatting | bytes 1310720 | tf_op jit(solution)/shard_map/all_to_all | solution.py:111
  183.1 15.4 %gather_fusion.1 = f32[1024,5,8]{2,1,0:T(8,128)} fusion(f32[5,8,32,128]{1,0,3,2:T(8,128)} %copy.54, s32[1024]{0:T(1024)S(1)} %bitcast.130), kind=kCustom, calls=%fused_computation.1 | custom fusion | bytes 335872 | tf_op jit(solution)/shard_map/gather | solution.py:112
  198.5 4.3 %fusion.4 = f32[5,1024]{0,1:T(8,128)} fusion(f32[1024,5,8]{2,1,0:T(8,128)} %gather_fusion.1, f32[8,1024]{0,1:T(8,128)} %copy.44), kind=kLoop, calls=%fused_computation.41 | loop fusion | flops 76800 | bytes 217088 | tf_op jit(solution)/shard_map/reduce_sum | solution.py:113
  202.8 7.6 %scatter_custom_fusion.1 = f32[5,2048]{0,1:T(8,128)S(1)} fusion(f32[5,2048]{0,1:T(8,128)S(1)} %bitcast.137, s32[1024]{0:T(1024)S(1)} %bitcast.147, f32[5,1024]{0,1:T(8,128)} %fusion.4, f32[5,2048]{0,1:T(8,128)S(1)} %bitcast.132, s32[1024]{0:T(1024)S(1)} %broadcast_clamp_fusion.1), kind=kCustom, calls=%fused_computation.44 | custom fusion | flops 5120 | bytes 1114112 | tf_op jit(solution)/shard_map/scatter | solution.py:119
  210.8 6.5 %while.81 = (s32[]{:T(128)}, f32[5,5,1024]{2,1,0:T(8,128)S(1)}, f32[5,1024]{1,0:T(8,128)S(1)}, s32[2]{0:T(128)S(1)}, f32[5,5,2,1024]{3,1,0,2:T(8,128)S(1)}, /*in...) while((s32[]{:T(128)}, f32[5,5,1024]{2,1,0:T(8,128)S(1)}, ...), condition=%wide.region_11.12_spmd, body=%wide.region_6.0_spmd.sunk | while | flops 558085 | bytes 1679519 | solution.py:43
  218.0 47.6 %while.82 = (s32[]{:T(128)}, f32[5,1024]{1,0:T(8,128)S(1)}, f32[5,1024]{1,0:T(8,128)}, f32[5,5,1024]{2,1,0:T(8,128)S(1)}, f32[5,1024]{1,0:T(8,128)S(1)}, /*index=5*/s32[]{:T(128)}) while((s32[]{:T(128)}, f32[5,1024]{1,0:T(8,128)S(1)}, f32[5,1024]{1,0:T(8,128)}, f32[5,5,1024]{2,1,0:T(8,128)S(1)}, f32[5,1024]{1,0:T(8,128)S(1)}, ...), condition=%wide.region_14.15_spmd, body=%wide.region_12.14_spmd.sunk | while | flops 51202 | bytes 368777 | solution.py:130
  218.0 3.3 collective-permute-start
  223.5 4.2 %collective-permute-start = (f32[5,1024]{1,0:T(8,128)S(1)}, f32[5,1024]{1,0:T(8,128)S(1)}, u32[]{:S(2)}, u32[]{:S(2)}) collective-permute-start(f32[5,1024]{1,0:T(8,128)S(1)} %get-tuple-element.881), channel_id=1, source_target_pairs={{0,4},{4,8},{8,12},{12,16},{16,20},{20,24},{24,28},{1,5},{5,9},{9,... | collective-permute-start | bytes 61448 | tf_op jit(solution)/shard_map/while/body/eval_jaxpr/ppermute | solution.py:12
  229.9 4.3 %collective-permute-start = (f32[5,1024]{1,0:T(8,128)S(1)}, f32[5,1024]{1,0:T(8,128)S(1)}, u32[]{:S(2)}, u32[]{:S(2)}) collective-permute-start(f32[5,1024]{1,0:T(8,128)S(1)} %get-tuple-element.881), channel_id=1, source_target_pairs={{0,4},{4,8},{8,12},{12,16},{16,20},{20,24},{24,28},{1,5},{5,9},{9,... | collective-permute-start | bytes 61448 | tf_op jit(solution)/shard_map/while/body/eval_jaxpr/ppermute | solution.py:12
  236.4 5.1 %collective-permute-start = (f32[5,1024]{1,0:T(8,128)S(1)}, f32[5,1024]{1,0:T(8,128)S(1)}, u32[]{:S(2)}, u32[]{:S(2)}) collective-permute-start(f32[5,1024]{1,0:T(8,128)S(1)} %get-tuple-element.881), channel_id=1, source_target_pairs={{0,4},{4,8},{8,12},{12,16},{16,20},{20,24},{24,28},{1,5},{5,9},{9,... | collective-permute-start | bytes 61448 | tf_op jit(solution)/shard_map/while/body/eval_jaxpr/ppermute | solution.py:12
  243.7 5.1 %collective-permute-start = (f32[5,1024]{1,0:T(8,128)S(1)}, f32[5,1024]{1,0:T(8,128)S(1)}, u32[]{:S(2)}, u32[]{:S(2)}) collective-permute-start(f32[5,1024]{1,0:T(8,128)S(1)} %get-tuple-element.881), channel_id=1, source_target_pairs={{0,4},{4,8},{8,12},{12,16},{16,20},{20,24},{24,28},{1,5},{5,9},{9,... | collective-permute-start | bytes 61448 | tf_op jit(solution)/shard_map/while/body/eval_jaxpr/ppermute | solution.py:12
  251.0 5.1 %collective-permute-start = (f32[5,1024]{1,0:T(8,128)S(1)}, f32[5,1024]{1,0:T(8,128)S(1)}, u32[]{:S(2)}, u32[]{:S(2)}) collective-permute-start(f32[5,1024]{1,0:T(8,128)S(1)} %get-tuple-element.881), channel_id=1, source_target_pairs={{0,4},{4,8},{8,12},{12,16},{16,20},{20,24},{24,28},{1,5},{5,9},{9,... | collective-permute-start | bytes 61448 | tf_op jit(solution)/shard_map/while/body/eval_jaxpr/ppermute | solution.py:12
  258.4 5.1 %collective-permute-start = (f32[5,1024]{1,0:T(8,128)S(1)}, f32[5,1024]{1,0:T(8,128)S(1)}, u32[]{:S(2)}, u32[]{:S(2)}) collective-permute-start(f32[5,1024]{1,0:T(8,128)S(1)} %get-tuple-element.881), channel_id=1, source_target_pairs={{0,4},{4,8},{8,12},{12,16},{16,20},{20,24},{24,28},{1,5},{5,9},{9,... | collective-permute-start | bytes 61448 | tf_op jit(solution)/shard_map/while/body/eval_jaxpr/ppermute | solution.py:12
  265.7 9.0 %while.83 = (s32[]{:T(128)}, f32[5,1024]{1,0:T(8,128)}, f32[2,5,1024]{2,1,0:T(8,128)S(1)}, s32[2]{0:T(128)S(1)}, f32[5,5,2,1024]{3,2,1,0:T(2,128)S(1)}, /*index=...) while((s32[]{:T(128)}, f32[5,1024]{1,0:T(8,128)}, ...), condition=%wide.region_18.19_spmd, body=%wide.region_15.18_spmd.sunk | while | flops 97285 | bytes 905403 | solution.py:57
  274.8 6.1 %while.86 = (s32[]{:T(128)}, f32[5,5,1024]{2,1,0:T(8,128)S(1)}, f32[5,1024]{1,0:T(8,128)S(1)}, s32[2]{0:T(128)S(1)}, f32[5,5,2,1024]{3,1,0,2:T(8,128)S(1)}, /*in...) while((s32[]{:T(128)}, f32[5,5,1024]{2,1,0:T(8,128)S(1)}, ...), condition=%wide.region_24.25_spmd.clone, body=%wide.region_19.24_spmd.clone.sunk | while | flops 563207 | bytes 1720501 | solution.py:74
  281.6 52.1 %while.84 = (s32[]{:T(128)}, f32[5,1024]{1,0:T(8,128)S(1)}, f32[5,1024]{1,0:T(8,128)}, f32[5,5,1024]{2,1,0:T(8,128)S(1)}, f32[5,1024]{1,0:T(8,128)S(1)}, /*index=5*/s32[]{:T(128)}) while((s32[]{:T(128)}, f32[5,1024]{1,0:T(8,128)S(1)}, f32[5,1024]{1,0:T(8,128)}, f32[5,5,1024]{2,1,0:T(8,128)S(1)}, f32[5,1024]{1,0:T(8,128)S(1)}, ...), condition=%wide.region_27.28_spmd, body=%wide.region_25.27_spmd.sunk | while | flops 51202 | bytes 368777 | solution.py:139
  282.9 5.7 %collective-permute-done.1 = f32[5,1024]{1,0:T(8,128)S(1)} collective-permute-done((f32[5,1024]{1,0:T(8,128)S(1)}, f32[5,1024]{1,0:T(8,128)S(1)}, u32[]{:S(2)}, u32[]{:S(2)}) %collective-permute-start.1) | collective-permute-done | bytes 20512 | tf_op jit(solution)/shard_map/while/body/eval_jaxpr/ppermute | solution.py:12
  290.5 5.7 %collective-permute-done.1 = f32[5,1024]{1,0:T(8,128)S(1)} collective-permute-done((f32[5,1024]{1,0:T(8,128)S(1)}, f32[5,1024]{1,0:T(8,128)S(1)}, u32[]{:S(2)}, u32[]{:S(2)}) %collective-permute-start.1) | collective-permute-done | bytes 20512 | tf_op jit(solution)/shard_map/while/body/eval_jaxpr/ppermute | solution.py:12
  298.1 5.4 %collective-permute-done.1 = f32[5,1024]{1,0:T(8,128)S(1)} collective-permute-done((f32[5,1024]{1,0:T(8,128)S(1)}, f32[5,1024]{1,0:T(8,128)S(1)}, u32[]{:S(2)}, u32[]{:S(2)}) %collective-permute-start.1) | collective-permute-done | bytes 20512 | tf_op jit(solution)/shard_map/while/body/eval_jaxpr/ppermute | solution.py:12
  305.4 5.5 %collective-permute-done.1 = f32[5,1024]{1,0:T(8,128)S(1)} collective-permute-done((f32[5,1024]{1,0:T(8,128)S(1)}, f32[5,1024]{1,0:T(8,128)S(1)}, u32[]{:S(2)}, u32[]{:S(2)}) %collective-permute-start.1) | collective-permute-done | bytes 20512 | tf_op jit(solution)/shard_map/while/body/eval_jaxpr/ppermute | solution.py:12
  312.8 5.6 %collective-permute-done.1 = f32[5,1024]{1,0:T(8,128)S(1)} collective-permute-done((f32[5,1024]{1,0:T(8,128)S(1)}, f32[5,1024]{1,0:T(8,128)S(1)}, u32[]{:S(2)}, u32[]{:S(2)}) %collective-permute-start.1) | collective-permute-done | bytes 20512 | tf_op jit(solution)/shard_map/while/body/eval_jaxpr/ppermute | solution.py:12
  320.3 5.4 %collective-permute-done.1 = f32[5,1024]{1,0:T(8,128)S(1)} collective-permute-done((f32[5,1024]{1,0:T(8,128)S(1)}, f32[5,1024]{1,0:T(8,128)S(1)}, u32[]{:S(2)}, u32[]{:S(2)}) %collective-permute-start.1) | collective-permute-done | bytes 20512 | tf_op jit(solution)/shard_map/while/body/eval_jaxpr/ppermute | solution.py:12
  327.6 5.4 %collective-permute-done.1 = f32[5,1024]{1,0:T(8,128)S(1)} collective-permute-done((f32[5,1024]{1,0:T(8,128)S(1)}, f32[5,1024]{1,0:T(8,128)S(1)}, u32[]{:S(2)}, u32[]{:S(2)}) %collective-permute-start.1) | collective-permute-done | bytes 20512 | tf_op jit(solution)/shard_map/while/body/eval_jaxpr/ppermute | solution.py:12
  333.7 9.4 %while.85 = (s32[]{:T(128)}, f32[5,1024]{1,0:T(8,128)}, f32[2,5,1024]{2,0,1:T(2,128)S(1)}, s32[2]{0:T(128)S(1)}, f32[2,5,1024]{2,1,0:T(8,128)S(1)}, /*index=5*/f...) while((s32[]{:T(128)}, f32[5,1024]{1,0:T(8,128)}, ...), condition=%wide.region_31.32_spmd, body=%wide.region_28.31_spmd.sunk | while | flops 102406 | bytes 901295 | solution.py:87
  (196 shorter events, 52.4 us)
Async XLA Ops:
  0.0 25.4 %copy-start.6 = (f32[5,2,1024]{2,1,0:T(2,128)S(1)}, f32[5,2,1024]{2,1,0:T(2,128)}, u32[]{:S(2)}) copy-start(f32[5,2,1024]{2,1,0:T(2,128)} %param.22) | copy-start | bytes 122884
  18.1 15.5 %all-to-all-start = ((s32[8,32,128]{2,0,1:T(8,128)}), s32[8,32,128]{2,0,1:T(8,128)S(1)}, u32[]{:S(2)}, u32[]{:S(2)}) async-start(s32[8,32,128]{2,0,1:T(8,128)} %copy.49), calls=%async_computation | async-start | bytes 262144 | tf_op jit(solution)/shard_map/all_to_all | solution.py:109
  141.9 13.9 %copy-start.9 = (f32[8,1024]{1,0:T(8,128)S(1)}, f32[8,1024]{1,0:T(8,128)}, u32[]{:S(2)}) copy-start(f32[8,1024]{1,0:T(8,128)} %param.30) | copy-start | bytes 98308
  141.9 14.9 %copy-start.7 = (f32[5,2,1024]{2,1,0:T(2,128)S(1)}, f32[5,2,1024]{2,1,0:T(2,128)}, u32[]{:S(2)}) copy-start(f32[5,2,1024]{2,1,0:T(2,128)} %param.23) | copy-start | bytes 122884
  141.9 15.2 %copy-start.2 = (f32[5,5,2,1024]{3,2,1,0:T(2,128)S(1)}, f32[5,5,2,1024]{3,2,1,0:T(2,128)}, u32[]{:S(2)}) copy-start(f32[5,5,2,1024]{3,2,1,0:T(2,128)} %param.24) | copy-start | bytes 614404
  141.9 15.3 %copy-start.10 = (s32[1,16]{1,0:T(1,128)S(1)}, s32[1,16]{1,0:T(1,128)}, u32[]{:S(2)}) copy-start(s32[1,16]{1,0:T(1,128)} %param.31) | copy-start | bytes 196
  152.4 21.2 %all-to-all-start.1 = ((f32[5,8,32,128]{3,1,0,2:T(8,128)}), f32[5,8,32,128]{3,1,0,2:T(8,128)}, u32[]{:S(2)}, u32[]{:S(2)}) async-start(f32[5,8,32,128]{3,1,0,2:T(8,128)} %bitcast.25), calls=%async_computation.1 | async-start | bytes 1310720 | tf_op jit(solution)/shard_map/all_to_all | solution.py:111
  198.5 12.4 %copy-start.3 = (f32[5,5,2,1024]{3,2,1,0:T(2,128)S(1)}, f32[5,5,2,1024]{3,2,1,0:T(2,128)}, u32[]{:S(2)}) copy-start(f32[5,5,2,1024]{3,2,1,0:T(2,128)} %param.25) | copy-start | bytes 614404
  217.4 57.4 %copy-start.4 = (f32[5,5,2,1024]{3,2,1,0:T(2,128)S(1)}, f32[5,5,2,1024]{3,2,1,0:T(2,128)}, u32[]{:S(2)}) copy-start(f32[5,5,2,1024]{3,2,1,0:T(2,128)} %param.26) | copy-start | bytes 614404
  218.0 4.9 %collective-permute-start = (f32[5,1024]{1,0:T(8,128)S(1)}, f32[5,1024]{1,0:T(8,128)S(1)}, u32[]{:S(2)}, u32[]{:S(2)}) collective-permute-start(f32[5,1024]{1,0:T(8,128)S(1)} %get-tuple-element.881), channel_id=1, source_target_pairs={{0,4},{4,8},{8,12},{12,16},{16,20},{20,24},{24,28},{1,5},{5,9},{9,... | collective-permute-start | bytes 61448 | tf_op jit(solution)/shard_map/while/body/eval_jaxpr/ppermute | solution.py:12
  223.5 5.8 %collective-permute-start = (f32[5,1024]{1,0:T(8,128)S(1)}, f32[5,1024]{1,0:T(8,128)S(1)}, u32[]{:S(2)}, u32[]{:S(2)}) collective-permute-start(f32[5,1024]{1,0:T(8,128)S(1)} %get-tuple-element.881), channel_id=1, source_target_pairs={{0,4},{4,8},{8,12},{12,16},{16,20},{20,24},{24,28},{1,5},{5,9},{9,... | collective-permute-start | bytes 61448 | tf_op jit(solution)/shard_map/while/body/eval_jaxpr/ppermute | solution.py:12
  229.9 5.9 %collective-permute-start = (f32[5,1024]{1,0:T(8,128)S(1)}, f32[5,1024]{1,0:T(8,128)S(1)}, u32[]{:S(2)}, u32[]{:S(2)}) collective-permute-start(f32[5,1024]{1,0:T(8,128)S(1)} %get-tuple-element.881), channel_id=1, source_target_pairs={{0,4},{4,8},{8,12},{12,16},{16,20},{20,24},{24,28},{1,5},{5,9},{9,... | collective-permute-start | bytes 61448 | tf_op jit(solution)/shard_map/while/body/eval_jaxpr/ppermute | solution.py:12
  236.4 6.7 %collective-permute-start = (f32[5,1024]{1,0:T(8,128)S(1)}, f32[5,1024]{1,0:T(8,128)S(1)}, u32[]{:S(2)}, u32[]{:S(2)}) collective-permute-start(f32[5,1024]{1,0:T(8,128)S(1)} %get-tuple-element.881), channel_id=1, source_target_pairs={{0,4},{4,8},{8,12},{12,16},{16,20},{20,24},{24,28},{1,5},{5,9},{9,... | collective-permute-start | bytes 61448 | tf_op jit(solution)/shard_map/while/body/eval_jaxpr/ppermute | solution.py:12
  243.7 6.7 %collective-permute-start = (f32[5,1024]{1,0:T(8,128)S(1)}, f32[5,1024]{1,0:T(8,128)S(1)}, u32[]{:S(2)}, u32[]{:S(2)}) collective-permute-start(f32[5,1024]{1,0:T(8,128)S(1)} %get-tuple-element.881), channel_id=1, source_target_pairs={{0,4},{4,8},{8,12},{12,16},{16,20},{20,24},{24,28},{1,5},{5,9},{9,... | collective-permute-start | bytes 61448 | tf_op jit(solution)/shard_map/while/body/eval_jaxpr/ppermute | solution.py:12
  251.0 6.7 %collective-permute-start = (f32[5,1024]{1,0:T(8,128)S(1)}, f32[5,1024]{1,0:T(8,128)S(1)}, u32[]{:S(2)}, u32[]{:S(2)}) collective-permute-start(f32[5,1024]{1,0:T(8,128)S(1)} %get-tuple-element.881), channel_id=1, source_target_pairs={{0,4},{4,8},{8,12},{12,16},{16,20},{20,24},{24,28},{1,5},{5,9},{9,... | collective-permute-start | bytes 61448 | tf_op jit(solution)/shard_map/while/body/eval_jaxpr/ppermute | solution.py:12
  258.4 6.7 %collective-permute-start = (f32[5,1024]{1,0:T(8,128)S(1)}, f32[5,1024]{1,0:T(8,128)S(1)}, u32[]{:S(2)}, u32[]{:S(2)}) collective-permute-start(f32[5,1024]{1,0:T(8,128)S(1)} %get-tuple-element.881), channel_id=1, source_target_pairs={{0,4},{4,8},{8,12},{12,16},{16,20},{20,24},{24,28},{1,5},{5,9},{9,... | collective-permute-start | bytes 61448 | tf_op jit(solution)/shard_map/while/body/eval_jaxpr/ppermute | solution.py:12
  269.6 0.6 copy-start.1
  274.1 0.6 copy-start.1
  281.6 7.0 %collective-permute-start.1 = (f32[5,1024]{1,0:T(8,128)S(1)}, f32[5,1024]{1,0:T(8,128)S(1)}, u32[]{:S(2)}, u32[]{:S(2)}) collective-permute-start(f32[5,1024]{1,0:T(8,128)S(1)} %get-tuple-element.959), channel_id=1, source_target_pairs={{4,0},{8,4},{12,8},{16,12},{20,16},{24,20},{28,24},{5,1},{9,5},{13... | collective-permute-start | bytes 61448 | tf_op jit(solution)/shard_map/while/body/eval_jaxpr/ppermute | solution.py:12
  288.6 0.6 copy-start.5
  289.2 7.0 %collective-permute-start.1 = (f32[5,1024]{1,0:T(8,128)S(1)}, f32[5,1024]{1,0:T(8,128)S(1)}, u32[]{:S(2)}, u32[]{:S(2)}) collective-permute-start(f32[5,1024]{1,0:T(8,128)S(1)} %get-tuple-element.959), channel_id=1, source_target_pairs={{4,0},{8,4},{12,8},{16,12},{20,16},{24,20},{28,24},{5,1},{9,5},{13... | collective-permute-start | bytes 61448 | tf_op jit(solution)/shard_map/while/body/eval_jaxpr/ppermute | solution.py:12
  296.2 0.6 copy-start.5
  296.8 6.7 %collective-permute-start.1 = (f32[5,1024]{1,0:T(8,128)S(1)}, f32[5,1024]{1,0:T(8,128)S(1)}, u32[]{:S(2)}, u32[]{:S(2)}) collective-permute-start(f32[5,1024]{1,0:T(8,128)S(1)} %get-tuple-element.959), channel_id=1, source_target_pairs={{4,0},{8,4},{12,8},{16,12},{20,16},{24,20},{28,24},{5,1},{9,5},{13... | collective-permute-start | bytes 61448 | tf_op jit(solution)/shard_map/while/body/eval_jaxpr/ppermute | solution.py:12
  303.5 0.6 copy-start.5
  304.1 6.8 %collective-permute-start.1 = (f32[5,1024]{1,0:T(8,128)S(1)}, f32[5,1024]{1,0:T(8,128)S(1)}, u32[]{:S(2)}, u32[]{:S(2)}) collective-permute-start(f32[5,1024]{1,0:T(8,128)S(1)} %get-tuple-element.959), channel_id=1, source_target_pairs={{4,0},{8,4},{12,8},{16,12},{20,16},{24,20},{28,24},{5,1},{9,5},{13... | collective-permute-start | bytes 61448 | tf_op jit(solution)/shard_map/while/body/eval_jaxpr/ppermute | solution.py:12
  310.9 0.6 copy-start.5
  311.5 6.9 %collective-permute-start.1 = (f32[5,1024]{1,0:T(8,128)S(1)}, f32[5,1024]{1,0:T(8,128)S(1)}, u32[]{:S(2)}, u32[]{:S(2)}) collective-permute-start(f32[5,1024]{1,0:T(8,128)S(1)} %get-tuple-element.959), channel_id=1, source_target_pairs={{4,0},{8,4},{12,8},{16,12},{20,16},{24,20},{28,24},{5,1},{9,5},{13... | collective-permute-start | bytes 61448 | tf_op jit(solution)/shard_map/while/body/eval_jaxpr/ppermute | solution.py:12
  318.4 0.6 copy-start.5
  319.0 6.7 %collective-permute-start.1 = (f32[5,1024]{1,0:T(8,128)S(1)}, f32[5,1024]{1,0:T(8,128)S(1)}, u32[]{:S(2)}, u32[]{:S(2)}) collective-permute-start(f32[5,1024]{1,0:T(8,128)S(1)} %get-tuple-element.959), channel_id=1, source_target_pairs={{4,0},{8,4},{12,8},{16,12},{20,16},{24,20},{28,24},{5,1},{9,5},{13... | collective-permute-start | bytes 61448 | tf_op jit(solution)/shard_map/while/body/eval_jaxpr/ppermute | solution.py:12
  325.7 0.6 copy-start.5
  326.4 6.7 %collective-permute-start.1 = (f32[5,1024]{1,0:T(8,128)S(1)}, f32[5,1024]{1,0:T(8,128)S(1)}, u32[]{:S(2)}, u32[]{:S(2)}) collective-permute-start(f32[5,1024]{1,0:T(8,128)S(1)} %get-tuple-element.959), channel_id=1, source_target_pairs={{4,0},{8,4},{12,8},{16,12},{20,16},{24,20},{28,24},{5,1},{9,5},{13... | collective-permute-start | bytes 61448 | tf_op jit(solution)/shard_map/while/body/eval_jaxpr/ppermute | solution.py:12
  343.0 0.6 copy-start.8
  (8 other events, 4.9 us)
where the time goes:
time: 345 us; the launch traced here: 344 us
  local copies, waits for them, and re-layouts  169 us (49%)
  waiting for transfers between devices  74 us (21%)
  starting transfers between devices  51.8 us (15%)
  other arithmetic  31.8 us (9%)
  loops' own time  17.1 us (5%)
    gather x2, local copies, waits for them, and re-layouts, body(): state_flat[:, lax.all_to_all(request, ('slab', 'cross'), split_axis=1, co...  119 us
    ppermute x14, waiting for transfers between devices, from_behind(): return lax.ppermute(array, axis, pairs)  49.8 us
    ppermute x14, starting transfers between devices, from_behind(): return lax.ppermute(array, axis, pairs)  41.2 us
    all_to_all x1, waiting for transfers between devices, body(): lax.all_to_all(found, ('slab', 'cross'), split_axis=2, concat_axis=2, til...  16.3 us
    gather x1, local copies, waits for them, and re-layouts, body(): picked = arrived[:, :, target, slot]  15.4 us
    all_to_all x1, local copies, waits for them, and re-layouts, body(): lax.all_to_all(found, ('slab', 'cross'), split_axis=2, concat_axis=2, til...  9.4 us
    another operation x4, other arithmetic  9.15 us
    while x36, local copies, waits for them, and re-layouts  8.81 us
  transfers between devices with their start and end apart: 16, of which 16 were waited for; matrix products, arithmetic and copies ran while one was open for 1% of the time, Pallas kernels for 0%

commit v1 on v0

v1 whole, which is shorter than its diff:
```python
import functools

import jax
import jax.numpy as jnp
from jax import lax
from jax.experimental import pallas as pl
from jax.experimental.pallas import tpu as pltpu
from jax.sharding import PartitionSpec as P

LANES = 128
MAT_ROWS = 80
VEC_ROWS = 16
MESH = pl.DeviceIdType.MESH


def kernel(
    dims,
    state,
    rhs,
    dinv,
    low,
    up,
    owner,
    donor,
    offsets,
    weights,
    perm,
    out,
    gath,
    onehot,
    mask,
    interp,
    mats,
    last,
    vecs,
    mrecv,
    brecv,
    solved,
    entry,
    g_send,
    g_recv,
    m_send,
    m_recv,
    b_send,
    b_recv,
    e_send,
    e_recv,
):
    nz, ny, nx, nc, width, tiles, fringe, corners = dims
    slabs = nz * ny
    solvers = min(tiles, slabs)
    apart = slabs // solvers
    rows = 2 * tiles
    s, c = lax.axis_index("slab"), lax.axis_index("cross")
    z, y = s // ny, lax.rem(s, ny)
    x, w = c // nc, lax.rem(c, nc)

    def at(slab, cross):
        return {"slab": slab, "cross": cross}

    stages = [
        (nz, lambda k: at(lax.rem(z + k, nz) * ny + y, c)),
        (ny, lambda k: at(z * ny + lax.rem(y + k, ny), c)),
        (nx, lambda k: at(s, lax.rem(x + k, nx) * nc + w)),
        (nc, lambda k: at(s, x * nc + lax.rem(w + k, nc))),
    ]

    barrier = pltpu.get_barrier_semaphore()
    peers = [at(lax.rem(s + k, slabs), c) for k in range(1, slabs)]
    for size, peer in stages[2:]:
        peers += [peer(k) for k in range(1, size)]
    for peer in peers:
        pl.semaphore_signal(barrier, inc=1, device_id=peer, device_id_type=MESH)
    pl.semaphore_wait(barrier, len(peers))

    starts = [0, nz, nz + ny, nz + ny + nx]
    views = [
        gath.at[z, y, x, w],
        gath.at[:, y, x, w],
        gath.at[:, :, x, w],
        gath.at[:, :, :, w],
    ]

    def send_stage(number):
        size, peer = stages[number]
        made = []
        for k in range(1, size):
            copy = pltpu.make_async_remote_copy(
                src_ref=state if number == 0 else views[number],
                dst_ref=views[number],
                send_sem=g_send.at[starts[number] + k],
                recv_sem=g_recv.at[starts[number] + k],
                device_id=peer(k),
                device_id_type=MESH,
            )
            copy.start()
            made.append(copy)
        return made

    def finish(made):
        for copy in made:
            copy.wait_recv()

    sent = [send_stage(0)]
    gath[z, y, x, w] = state[...]

    def cell(ref, i, j, p):
        return ref[pl.ds((i * width + j) * rows + p, tiles, stride=2), :]

    def block(ref, p):
        return [[cell(ref, i, j, p) for j in range(width)] for i in range(width)]

    def product(a, b):
        return [
            [sum(a[i][k] * b[k][j] for k in range(width)) for j in range(width)]
            for i in range(width)
        ]

    def keep(ref, stride, base, value):
        ref[pl.ds(base, tiles, stride=stride), :] = value

    def keep_block(number, a):
        for i in range(width):
            for j in range(width):
                keep(mats, MAT_ROWS, number * width * width + j * width + i, a[i][j])

    first_low = product(block(dinv, 0), block(low, 0))
    both_low = product(product(block(dinv, 1), block(low, 1)), first_low)
    keep_block(0, both_low)
    first_up = product(block(dinv, 0), block(up, 0))
    through = product(first_up, both_low)
    keep_block(
        1, [[first_low[i][j] + through[i][j] for j in range(width)] for i in range(width)]
    )
    last_up = product(block(dinv, 1), block(up, 1))
    for i in range(width):
        for j in range(width):
            last[i * width + j] = last_up[i][j]
    keep_block(2, product(first_up, last_up))
    for chunk in range(tiles):
        mats[pl.ds(chunk * MAT_ROWS + 3 * width * width, 5), :] = jnp.zeros(
            (5, LANES), jnp.float32
        )

    def for_solver(act):
        if apart == 1:
            act()
        else:
            pl.when(lax.rem(s, apart) == 0)(act)

    def to_solver(k, source, size, landing, send, receive):
        chunk = lax.rem(s // apart + k, solvers)
        return pltpu.make_async_remote_copy(
            src_ref=source.at[pl.ds(pl.multiple_of(chunk * size, 8), size)],
            dst_ref=landing.at[s],
            send_sem=send.at[k],
            recv_sem=receive.at[s],
            device_id=at(chunk * apart, c),
            device_id_type=MESH,
        )

    def scatter(act, source, size, landing, send, receive):
        for k in range(1, solvers):
            act(to_solver(k, source, size, landing, send, receive))
        if apart > 1:

            @pl.when(lax.rem(s, apart) != 0)
            def _():
                act(to_solver(0, source, size, landing, send, receive))

    def own_chunk(source, size, landing):
        def act():
            own = pl.multiple_of((s // apart) * size, 8)
            landing[s] = source[pl.ds(own, size), :]

        for_solver(act)

    def arrivals(landing, receive):
        for k in range(1, slabs):
            sender = lax.rem(s + k, slabs)
            pltpu.make_async_remote_copy(
                src_ref=landing.at[sender],
                dst_ref=landing.at[sender],
                send_sem=receive.at[sender],
                recv_sem=receive.at[sender],
                device_id=at(sender, c),
                device_id_type=MESH,
            ).wait_recv()

    scatter(lambda copy: copy.start(), mats, MAT_ROWS, mrecv, m_send, m_recv)
    own_chunk(mats, MAT_ROWS, mrecv)

    finish(sent[0])
    sent.append(send_stage(1))

    def fill_mask(i, carry):
        at_cell = lax.broadcasted_iota(jnp.int32, (8, fringe), 0) + i * 8
        total = jnp.zeros((8, fringe), jnp.float32)
        for k in range(corners):
            hit = at_cell == offsets[k : k + 1, :]
            total = total + jnp.where(hit, weights[k : k + 1, :], 0.0)
        mask[pl.ds(pl.multiple_of(i * 8, 8), 8), :] = total
        return carry

    lax.fori_loop(0, LANES // 8, fill_mask, 0)
    finish(sent[1])
    sent.append(send_stage(2))

    blocks = donor[...]
    wanted = owner[...] * rows + (blocks % tiles) * 2 + blocks // tiles

    def fill_onehot(i, carry):
        number = lax.broadcasted_iota(jnp.int32, (16, fringe), 0) + i * 16
        value = jnp.where(number == wanted, 1.0, 0.0).astype(jnp.bfloat16)
        onehot[pl.ds(pl.multiple_of(i * 16, 16), 16), :] = value
        return carry

    count = nz * ny * nx * nc * rows
    lax.fori_loop(0, count // 16, fill_onehot, 0)
    finish(sent[2])
    sent.append(send_stage(3))
    finish(sent[3])

    def interpolate(v, carry):
        table = gath[:, :, :, :, pl.ds(pl.multiple_of(v * rows, 8), rows), :]
        table = table.reshape(count, LANES)
        high = table.astype(jnp.bfloat16)
        rest = (table - high.astype(jnp.float32)).astype(jnp.bfloat16)
        both = jnp.concatenate([high, rest], axis=1)
        picked = lax.dot_general(
            both, onehot[...], (((0,), (0,)), ((), ())), preferred_element_type=jnp.float32
        )
        picked = (picked[:LANES] + picked[LANES:]) * mask[...]
        row = jnp.sum(picked, axis=0, keepdims=True)
        for j in range(fringe // LANES):
            interp[v, j : j + 1, :] = row[:, j * LANES : (j + 1) * LANES]
        return carry

    lax.fori_loop(0, width, interpolate, 0)

    tile = lax.broadcasted_iota(jnp.int32, (tiles, LANES), 0)
    forcing = [[], []]
    for v in range(width):
        fresh = interp[v]
        for p in range(2):
            there = pl.ds(v * rows + p, tiles, stride=2)
            now, value = state[there, :], rhs[there, :]
            for j in range(fringe // LANES):
                hit = tile + p * tiles == perm[0, j]
                value = jnp.where(hit, fresh[j : j + 1, :] - now, value)
            forcing[p].append(value)

    def apply(a, b):
        return [sum(a(i, j) * b[j] for j in range(width)) for i in range(width)]

    def plus(a, b):
        return [i + j for i, j in zip(a, b)]

    def of(ref, p):
        return lambda i, j: cell(ref, i, j, p)

    def kept(number):
        return lambda i, j: mats[
            pl.ds(number * width * width + j * width + i, tiles, stride=MAT_ROWS), :
        ]

    lower_first = apply(of(dinv, 0), forcing[0])
    lower_last = apply(of(dinv, 1), plus(forcing[1], apply(of(low, 1), lower_first)))
    upper_first = plus(lower_first, apply(of(dinv, 0), apply(of(up, 0), lower_last)))
    vecs[...] = jnp.zeros_like(vecs)
    for i in range(width):
        keep(vecs, VEC_ROWS, i, lower_last[i])
        keep(vecs, VEC_ROWS, 8 + i, upper_first[i])
    scatter(lambda copy: copy.start(), vecs, VEC_ROWS, brecv, b_send, b_recv)
    own_chunk(vecs, VEC_ROWS, brecv)

    def to_owner(k):
        target = lax.rem(s + k, slabs)
        return pltpu.make_async_remote_copy(
            src_ref=solved.at[target],
            dst_ref=entry.at[pl.ds(pl.multiple_of((s // apart) * VEC_ROWS, 8), VEC_ROWS)],
            send_sem=e_send.at[k],
            recv_sem=e_recv.at[s // apart],
            device_id=at(target, c),
            device_id_type=MESH,
        )

    def solve():
        arrivals(mrecv, m_recv)
        arrivals(brecv, b_recv)

        def matvec(slab, number, vector):
            base = number * width * width
            return sum(
                mrecv[slab, base + j * width : base + (j + 1) * width, :] * vector[j : j + 1, :]
                for j in range(width)
            )

        solved[...] = jnp.zeros_like(solved)
        value = jnp.zeros((width, LANES), jnp.float32)
        constants = []
        for slab in range(slabs):
            solved[slab, 0:width, :] = value
            constants.append(brecv[slab, 8 : 8 + width, :] + matvec(slab, 1, value))
            value = brecv[slab, 0:width, :] + matvec(slab, 0, value)
        value = jnp.zeros((width, LANES), jnp.float32)
        for slab in reversed(range(slabs)):
            solved[slab, 8 : 8 + width, :] = value
            value = constants[slab] + matvec(slab, 2, value)
        for k in range(1, slabs):
            to_owner(k).start()
        own = pl.multiple_of((s // apart) * VEC_ROWS, 8)
        entry[pl.ds(own, VEC_ROWS), :] = solved[s]

    for_solver(solve)

    def take(j):
        there = entry.at[pl.ds(pl.multiple_of(j * VEC_ROWS, 8), VEC_ROWS)]
        pltpu.make_async_remote_copy(
            src_ref=there,
            dst_ref=there,
            send_sem=e_recv.at[j],
            recv_sem=e_recv.at[j],
            device_id=at(j * apart, c),
            device_id_type=MESH,
        ).wait_recv()

    for k in range(1, solvers):
        take(lax.rem(s // apart + k, solvers))
    if apart > 1:
        pl.when(lax.rem(s, apart) != 0)(lambda: take(s // apart))

    def entries(base):
        return [entry[pl.ds(base + i, tiles, stride=VEC_ROWS), :] for i in range(width)]

    from_below, from_above = entries(0), entries(8)
    result_first = plus(
        upper_first, plus(apply(kept(1), from_below), apply(kept(2), from_above))
    )
    result_last = plus(
        lower_last,
        plus(
            apply(kept(0), from_below),
            apply(lambda i, j: last[i * width + j], from_above),
        ),
    )
    for v in range(width):
        out[pl.ds(v * rows, tiles, stride=2), :] = result_first[v]
        out[pl.ds(v * rows + 1, tiles, stride=2), :] = result_last[v]

    for made in sent:
        for copy in made:
            copy.wait_send()
    scatter(lambda copy: copy.wait_send(), mats, MAT_ROWS, mrecv, m_send, m_recv)
    scatter(lambda copy: copy.wait_send(), vecs, VEC_ROWS, brecv, b_send, b_recv)

    def drain():
        for k in range(1, slabs):
            to_owner(k).wait_send()

    for_solver(drain)


def by_tile(array):
    planes, cells = array.shape[-2:]
    split = array.reshape(-1, planes, cells // LANES, LANES)
    return jnp.swapaxes(split, 1, 2).reshape(-1, LANES)


def body(
    state, rhs, dinv, lower_jac, upper_jac, owner, donor_block, offsets, weights, receptor_perm
):
    width, planes, cells = state.shape
    assert planes == 2 and cells % LANES == 0
    slabs, crosses = lax.axis_size("slab"), lax.axis_size("cross")
    ny = 2 if slabs % 2 == 0 else 1
    nc = 2 if crosses % 2 == 0 else 1
    nz, nx = slabs // ny, crosses // nc
    tiles = cells // LANES
    solvers = min(tiles, slabs)
    assert solvers == tiles and slabs % solvers == 0
    rows = planes * tiles
    corners, fringe = offsets.shape
    dims = (nz, ny, nx, nc, width, tiles, fringe, corners)
    f32 = jnp.float32
    vmem = pl.BlockSpec(memory_space=pltpu.VMEM)
    dma = pltpu.SemaphoreType.DMA
    made = pl.pallas_call(
        functools.partial(kernel, dims),
        out_shape=jax.ShapeDtypeStruct((width * rows, LANES), f32),
        in_specs=[vmem] * 9 + [pl.BlockSpec(memory_space=pltpu.SMEM)],
        out_specs=vmem,
        scratch_shapes=[
            pltpu.VMEM((nz, ny, nx, nc, width * rows, LANES), f32),
            pltpu.VMEM((slabs * crosses * rows, fringe), jnp.bfloat16),
            pltpu.VMEM((LANES, fringe), f32),
            pltpu.VMEM((width, fringe // LANES, LANES), f32),
            pltpu.VMEM((tiles * MAT_ROWS, LANES), f32),
            pltpu.VMEM((width * width, tiles, LANES), f32),
            pltpu.VMEM((tiles * VEC_ROWS, LANES), f32),
            pltpu.VMEM((slabs, MAT_ROWS, LANES), f32),
            pltpu.VMEM((slabs, VEC_ROWS, LANES), f32),
            pltpu.VMEM((slabs, VEC_ROWS, LANES), f32),
            pltpu.VMEM((tiles * VEC_ROWS, LANES), f32),
            dma((nz + ny + nx + nc,)),
            dma((nz + ny + nx + nc,)),
            dma((solvers,)),
            dma((slabs,)),
            dma((solvers,)),
            dma((slabs,)),
            dma((slabs,)),
            dma((solvers,)),
        ],
        compiler_params=pltpu.CompilerParams(
            collective_id=0, has_side_effects=True, vmem_limit_bytes=40 * 2**20
        ),
    )(
        by_tile(state),
        by_tile(rhs),
        by_tile(dinv),
        by_tile(lower_jac),
        by_tile(upper_jac),
        owner.reshape(1, fringe),
        donor_block.reshape(1, fringe),
        offsets,
        weights,
        receptor_perm,
    )
    made = jnp.swapaxes(made.reshape(width, tiles, planes, LANES), 1, 2)
    return made.reshape(width, planes, cells)


def solution(mesh):
    whole = ("slab", "cross")
    return jax.shard_map(
        body,
        mesh=mesh,
        in_specs=(
            P(None, "slab", "cross"),
            P(None, "slab", "cross"),
            P(None, None, "slab", "cross"),
            P(None, None, "slab", "cross"),
            P(None, None, "slab", "cross"),
            P(whole, None),
            P(whole),
            P(None, whole),
            P(None, whole),
            P(whole, None),
        ),
        out_specs=P(None, "slab", "cross"),
        check_vma=False,
    )
```

time: 345 us -> 45.1 us (0.13)
  local copies, waits for them, and re-layouts: 169 us -> 7.18 us
  waiting for transfers between devices: 74 us -> 0 us
  starting transfers between devices: 51.8 us -> 0 us
  Pallas kernels: 0 us -> 37.4 us
  other arithmetic: 31.8 us -> 0 us
  loops' own time: 17.1 us -> 0 us
    gather x3 -> x0, local copies, waits for them, and re-layouts: 134 us -> none  [the longest x2 119 us: body(): state_flat[:, lax.all_to_all(request, ('slab', 'cross'), split_axis=1, co...]
    ppermute x14 -> x0, waiting for transfers between devices: 49.8 us -> none  [from_behind(): return lax.ppermute(array, axis, pairs)]
    ppermute x14 -> x0, starting transfers between devices: 41.2 us -> none  [from_behind(): return lax.ppermute(array, axis, pairs)]
    pallas_call x0 -> x1, Pallas kernels: none -> 37.4 us  [body(): pl.pallas_call(functools.partial(kernel, dims), out_shape=jax.ShapeDtypeS...]
    all_to_all x2 -> x0, waiting for transfers between devices: 24.1 us -> none  [the longest x1 16.3 us: body(): lax.all_to_all(found, ('slab', 'cross'), split_axis=2, concat_axis=2, til...]
    another operation x6 -> x0, loops' own time: 17.1 us -> none  [the longest x1 4.3 us: lower_digest_state(): result, _ = lax.scan(step, start, jnp.arange(planes))]
    all_to_all x2 -> x0, starting transfers between devices: 10.6 us -> none  [the longest x1 7.3 us: body(): lax.all_to_all(request, ('slab', 'cross'), split_axis=1, concat_axis=1, t...]
    reduce_sum x40 -> x0, other arithmetic: 10.6 us -> none  [the longest x30 4.87 us: apply_block(): return jnp.sum(matrix * vector[None], axis=1)]
  transfers between devices with their start and end apart: 16 -> 0, of which waited for: 16 -> 0; matrix products, arithmetic and copies ran while one was open for 1% -> 0% of each run, Pallas kernels for 0% -> 0%
where the time goes in v1:
time: 45.1 us; the launch traced here: 44.6 us
  Pallas kernels  37.4 us (83%)
  local copies, waits for them, and re-layouts  7.18 us (16%)
    pallas_call x1, Pallas kernels, body(): pl.pallas_call(functools.partial(kernel, dims), out_shape=jax.ShapeDtypeS...  37.4 us
    unnamed x21, local copies, waits for them, and re-layouts  7.18 us

profile of v1, /device:TPU:0, one launch (start us, length us, event | category | flops | bytes accessed | tf_op | source)
XLA Modules:
  0.0 44.6 jit_solution(1936052437354015473)
XLA Ops:
  0.0 0.0 copy-start.8
  0.0 0.0 copy-start.7
  0.0 0.0 copy-start.9
  0.0 0.7 %copy-done.8 = s32[1024]{0:T(1024)S(1)} copy-done((s32[1024]{0:T(1024)S(1)}, s32[1024]{0:T(1024)}, u32[]{:S(2)}) %copy-start.8) | copy-done | bytes 4120
  0.7 0.0 copy-done.7
  0.7 0.0 copy-done.9
  0.7 0.0 copy-start
  0.7 0.9 %copy-done = f32[5,5,2,1024]{3,2,1,0:T(2,128)S(1)} copy-done((f32[5,5,2,1024]{3,2,1,0:T(2,128)S(1)}, f32[5,5,2,1024]{3,2,1,0:T(2,128)}, u32[]{:S(2)}) %copy-start) | copy-done | bytes 204824
  1.6 0.0 copy-start.1
  1.6 0.9 %copy-done.1 = f32[5,5,2,1024]{3,2,1,0:T(2,128)S(1)} copy-done((f32[5,5,2,1024]{3,2,1,0:T(2,128)S(1)}, f32[5,5,2,1024]{3,2,1,0:T(2,128)}, u32[]{:S(2)}) %copy-start.1) | copy-done | bytes 204824
  2.6 0.0 copy-start.2
  2.6 0.9 %copy-done.2 = f32[5,5,2,1024]{3,2,1,0:T(2,128)S(1)} copy-done((f32[5,5,2,1024]{3,2,1,0:T(2,128)S(1)}, f32[5,5,2,1024]{3,2,1,0:T(2,128)}, u32[]{:S(2)}) %copy-start.2) | copy-done | bytes 204824
  3.5 0.0 copy-start.3
  3.5 0.8 %copy-done.3 = f32[5,2,1024]{2,1,0:T(2,128)S(1)} copy-done((f32[5,2,1024]{2,1,0:T(2,128)S(1)}, f32[5,2,1024]{2,1,0:T(2,128)}, u32[]{:S(2)}) %copy-start.3) | copy-done | bytes 40984
  4.3 0.0 copy-start.4
  4.3 0.8 %copy-done.4 = f32[5,2,1024]{2,1,0:T(2,128)S(1)} copy-done((f32[5,2,1024]{2,1,0:T(2,128)S(1)}, f32[5,2,1024]{2,1,0:T(2,128)}, u32[]{:S(2)}) %copy-start.4) | copy-done | bytes 40984
  5.1 0.0 copy-start.5
  5.1 0.8 %copy-done.5 = s32[8,1024]{1,0:T(8,128)S(1)} copy-done((s32[8,1024]{1,0:T(8,128)S(1)}, s32[8,1024]{1,0:T(8,128)}, u32[]{:S(2)}) %copy-start.5) | copy-done | bytes 32792
  5.8 0.0 copy-start.6
  5.8 0.8 %copy-done.6 = f32[8,1024]{1,0:T(8,128)S(1)} copy-done((f32[8,1024]{1,0:T(8,128)S(1)}, f32[8,1024]{1,0:T(8,128)}, u32[]{:S(2)}) %copy-start.6) | copy-done | bytes 32792
  6.6 37.4 %shard_map.100 = f32[80,128]{1,0:T(8,128)S(1)} custom-call(f32[80,128]{1,0:T(8,128)S(1)} %bitcast.36, f32[80,128]{1,0:T(8,128)S(1)} %bitcast.37, f32[400,128]{1,0:T(8,128)S(1)} %bitcast.32, f32[400,128]{1,0:T(8,128)S(1)} %bitcast.33, f32[400,128]{1,0:T(8,128)S(1)} %bitcast.34, s32[1,1024]{1,0:T(1,128)S(1)} %bitcast.38, s32[1,1024]{1,0:T(1,128)S(1)} %bitcast.39, ...), custom_call_target="tpu_custom_call" | custom-call | tf_op jit(solution)/shard_map/pallas_call | solution.py:388
  44.0 0.6 %copy.18 = f32[5,2,1024]{2,1,0:T(2,128)} copy(f32[5,2,1024]{2,1,0:T(2,128)S(1)} %bitcast.35) | data formatting | bytes 81920
Async XLA Ops:
  0.0 0.7 %copy-start.8 = (s32[1024]{0:T(1024)S(1)}, s32[1024]{0:T(1024)}, u32[]{:S(2)}) copy-start(s32[1024]{0:T(1024)} %param.16) | copy-start | bytes 12292
  0.0 0.7 %copy-start.7 = (s32[1024,1]{0,1:T(1,128)S(1)}, s32[1024,1]{0,1:T(1,128)}, u32[]{:S(2)}) copy-start(s32[1024,1]{0,1:T(1,128)} %param.15) | copy-start | bytes 12292
  0.0 0.7 %copy-start.9 = (s32[1,16]{1,0:T(1,128)S(1)}, s32[1,16]{1,0:T(1,128)}, u32[]{:S(2)}) copy-start(s32[1,16]{1,0:T(1,128)} %perm.1) | copy-start | bytes 196
  0.7 0.9 %copy-start = (f32[5,5,2,1024]{3,2,1,0:T(2,128)S(1)}, f32[5,5,2,1024]{3,2,1,0:T(2,128)}, u32[]{:S(2)}) copy-start(f32[5,5,2,1024]{3,2,1,0:T(2,128)} %param.12) | copy-start | bytes 614404
  1.6 0.9 %copy-start.1 = (f32[5,5,2,1024]{3,2,1,0:T(2,128)S(1)}, f32[5,5,2,1024]{3,2,1,0:T(2,128)}, u32[]{:S(2)}) copy-start(f32[5,5,2,1024]{3,2,1,0:T(2,128)} %param.13) | copy-start | bytes 614404
  2.6 0.9 %copy-start.2 = (f32[5,5,2,1024]{3,2,1,0:T(2,128)S(1)}, f32[5,5,2,1024]{3,2,1,0:T(2,128)}, u32[]{:S(2)}) copy-start(f32[5,5,2,1024]{3,2,1,0:T(2,128)} %param.14) | copy-start | bytes 614404
  3.5 0.8 %copy-start.3 = (f32[5,2,1024]{2,1,0:T(2,128)S(1)}, f32[5,2,1024]{2,1,0:T(2,128)}, u32[]{:S(2)}) copy-start(f32[5,2,1024]{2,1,0:T(2,128)} %param.10) | copy-start | bytes 122884
  4.3 0.8 %copy-start.4 = (f32[5,2,1024]{2,1,0:T(2,128)S(1)}, f32[5,2,1024]{2,1,0:T(2,128)}, u32[]{:S(2)}) copy-start(f32[5,2,1024]{2,1,0:T(2,128)} %param.11) | copy-start | bytes 122884
  5.1 0.8 %copy-start.5 = (s32[8,1024]{1,0:T(8,128)S(1)}, s32[8,1024]{1,0:T(8,128)}, u32[]{:S(2)}) copy-start(s32[8,1024]{1,0:T(8,128)} %offsets.1) | copy-start | bytes 98308
  5.8 0.8 %copy-start.6 = (f32[8,1024]{1,0:T(8,128)S(1)}, f32[8,1024]{1,0:T(8,128)}, u32[]{:S(2)}) copy-start(f32[8,1024]{1,0:T(8,128)} %weights.1) | copy-start | bytes 98308

commit v2 on v1

--- a/solution.py
+++ b/solution.py
@@ -15,17 +15,12 @@
 
 def kernel(
     dims,
-    state,
-    rhs,
-    dinv,
-    low,
-    up,
-    owner,
-    donor,
-    offsets,
-    weights,
-    perm,
-    out,
+    *refs,
+):
+    sources, (out,), scratch = refs[:10], refs[10:11], refs[11:]
+    held, f_sem, scratch = scratch[:10], scratch[10], scratch[11:]
+    state, rhs, dinv, low, up, owner, donor, offsets, weights, perm = held
+    (
     gath,
     onehot,
     mask,
@@ -45,7 +40,7 @@
     b_recv,
     e_send,
     e_recv,
-):
+    ) = scratch
     nz, ny, nx, nc, width, tiles, fringe, corners = dims
     slabs = nz * ny
     solvers = min(tiles, slabs)
@@ -58,51 +53,58 @@
     def at(slab, cross):
         return {"slab": slab, "cross": cross}
 
-    stages = [
-        (nz, lambda k: at(lax.rem(z + k, nz) * ny + y, c)),
-        (ny, lambda k: at(z * ny + lax.rem(y + k, ny), c)),
-        (nx, lambda k: at(s, lax.rem(x + k, nx) * nc + w)),
-        (nc, lambda k: at(s, x * nc + lax.rem(w + k, nc))),
+    z_peer = lambda k: at(lax.rem(z + k, nz) * ny + y, c)
+    y_peer = lambda k: at(z * ny + lax.rem(y + k, ny), c)
+    x_peer = lambda k: at(s, lax.rem(x + k, nx) * nc + w)
+    w_peer = lambda k: at(s, x * nc + lax.rem(w + k, nc))
+
+    fetches = [
+        pltpu.make_async_copy(source, target, f_sem.at[number])
+        for number, (source, target) in enumerate(zip(sources, held))
     ]
+    for fetch in fetches:
+        fetch.start()
 
     barrier = pltpu.get_barrier_semaphore()
     peers = [at(lax.rem(s + k, slabs), c) for k in range(1, slabs)]
-    for size, peer in stages[2:]:
-        peers += [peer(k) for k in range(1, size)]
+    peers += [x_peer(k) for k in range(1, nx)] + [w_peer(k) for k in range(1, nc)]
     for peer in peers:
         pl.semaphore_signal(barrier, inc=1, device_id=peer, device_id_type=MESH)
+    fetches[0].wait()
     pl.semaphore_wait(barrier, len(peers))
 
-    starts = [0, nz, nz + ny, nz + ny + nx]
-    views = [
-        gath.at[z, y, x, w],
-        gath.at[:, y, x, w],
-        gath.at[:, :, x, w],
-        gath.at[:, :, :, w],
-    ]
-
-    def send_stage(number):
-        size, peer = stages[number]
+    half = width * rows // 2
+    first, second = pl.ds(0, half), pl.ds(half, half)
+    sent = []
+
+    def send(size, peer, source, landing):
         made = []
         for k in range(1, size):
+            slot = len(sent)
             copy = pltpu.make_async_remote_copy(
-                src_ref=state if number == 0 else views[number],
-                dst_ref=views[number],
-                send_sem=g_send.at[starts[number] + k],
-                recv_sem=g_recv.at[starts[number] + k],
+                src_ref=source,
+                dst_ref=landing,
+                send_sem=g_send.at[slot],
+                recv_sem=g_recv.at[slot],
                 device_id=peer(k),
                 device_id_type=MESH,
             )
             copy.start()
             made.append(copy)
+            sent.append(copy)
         return made
+
+    def pass_on(size, peer, view):
+        return send(size, peer, view, view)
 
     def finish(made):
         for copy in made:
             copy.wait_recv()
 
-    sent = [send_stage(0)]
-    gath[z, y, x, w] = state[...]
+    along_z = send(nz, z_peer, state, gath.at[w, z, y, x])
+    gath[w, z, y, x] = state[...]
+    for fetch in fetches[1:5]:
+        fetch.wait()
 
     def cell(ref, i, j, p):
         return ref[pl.ds((i * width + j) * rows + p, tiles, stride=2), :]
@@ -187,11 +189,13 @@
                 device_id_type=MESH,
             ).wait_recv()
 
-    scatter(lambda copy: copy.start(), mats, MAT_ROWS, mrecv, m_send, m_recv)
     own_chunk(mats, MAT_ROWS, mrecv)
 
-    finish(sent[0])
-    sent.append(send_stage(1))
+    finish(along_z)
+    first_y = pass_on(ny, y_peer, gath.at[w, :, y, x, first])
+    second_x = pass_on(nx, x_peer, gath.at[w, :, y, x, second])
+    for fetch in fetches[5:]:
+        fetch.wait()
 
     def fill_mask(i, carry):
         at_cell = lax.broadcasted_iota(jnp.int32, (8, fringe), 0) + i * 8
@@ -203,11 +207,16 @@
         return carry
 
     lax.fori_loop(0, LANES // 8, fill_mask, 0)
-    finish(sent[1])
-    sent.append(send_stage(2))
+    finish(first_y)
+    first_x = pass_on(nx, x_peer, gath.at[w, :, :, x, first])
+    finish(second_x)
+    second_y = pass_on(ny, y_peer, gath.at[w, :, y, :, second])
+    scatter(lambda copy: copy.start(), mats, MAT_ROWS, mrecv, m_send, m_recv)
 
     blocks = donor[...]
-    wanted = owner[...] * rows + (blocks % tiles) * 2 + blocks // tiles
+    group = nz * ny * nx
+    place = (owner[...] % nc) * group + owner[...] // nc
+    wanted = place * rows + (blocks % tiles) * 2 + blocks // tiles
 
     def fill_onehot(i, carry):
         number = lax.broadcasted_iota(jnp.int32, (16, fringe), 0) + i * 16
@@ -217,26 +226,35 @@
 
     count = nz * ny * nx * nc * rows
     lax.fori_loop(0, count // 16, fill_onehot, 0)
-    finish(sent[2])
-    sent.append(send_stage(3))
-    finish(sent[3])
-
-    def interpolate(v, carry):
-        table = gath[:, :, :, :, pl.ds(pl.multiple_of(v * rows, 8), rows), :]
-        table = table.reshape(count, LANES)
+    finish(second_y)
+    by_core = pass_on(nc, w_peer, gath.at[w, :, :, :, second])
+    finish(first_x)
+    by_core += pass_on(nc, w_peer, gath.at[w, :, :, :, first])
+
+    part = group * rows
+
+    def interpolate(core, add, v, carry):
+        table = gath[core, :, :, :, pl.ds(pl.multiple_of(v * rows, 8), rows), :]
+        table = table.reshape(part, LANES)
         high = table.astype(jnp.bfloat16)
         rest = (table - high.astype(jnp.float32)).astype(jnp.bfloat16)
+        chosen = onehot[pl.ds(pl.multiple_of(core * part, 16), part), :]
         both = jnp.concatenate([high, rest], axis=1)
         picked = lax.dot_general(
-            both, onehot[...], (((0,), (0,)), ((), ())), preferred_element_type=jnp.float32
+            both, chosen, (((0,), (0,)), ((), ())), preferred_element_type=jnp.float32
         )
         picked = (picked[:LANES] + picked[LANES:]) * mask[...]
         row = jnp.sum(picked, axis=0, keepdims=True)
         for j in range(fringe // LANES):
-            interp[v, j : j + 1, :] = row[:, j * LANES : (j + 1) * LANES]
+            value = row[:, j * LANES : (j + 1) * LANES]
+            interp[v, j : j + 1, :] = interp[v, j : j + 1, :] + value if add else value
         return carry
 
-    lax.fori_loop(0, width, interpolate, 0)
+    lax.fori_loop(0, width, functools.partial(interpolate, w, False), 0)
+    finish(by_core)
+    for k in range(1, nc):
+        core = lax.rem(w + k, nc)
+        lax.fori_loop(0, width, functools.partial(interpolate, core, True), 0)
 
     tile = lax.broadcasted_iota(jnp.int32, (tiles, LANES), 0)
     forcing = [[], []]
@@ -348,9 +366,8 @@
         out[pl.ds(v * rows, tiles, stride=2), :] = result_first[v]
         out[pl.ds(v * rows + 1, tiles, stride=2), :] = result_last[v]
 
-    for made in sent:
-        for copy in made:
-            copy.wait_send()
+    for copy in sent:
+        copy.wait_send()
     scatter(lambda copy: copy.wait_send(), mats, MAT_ROWS, mrecv, m_send, m_recv)
     scatter(lambda copy: copy.wait_send(), vecs, VEC_ROWS, brecv, b_send, b_recv)
 
@@ -385,36 +402,8 @@
     f32 = jnp.float32
     vmem = pl.BlockSpec(memory_space=pltpu.VMEM)
     dma = pltpu.SemaphoreType.DMA
-    made = pl.pallas_call(
-        functools.partial(kernel, dims),
-        out_shape=jax.ShapeDtypeStruct((width * rows, LANES), f32),
-        in_specs=[vmem] * 9 + [pl.BlockSpec(memory_space=pltpu.SMEM)],
-        out_specs=vmem,
-        scratch_shapes=[
-            pltpu.VMEM((nz, ny, nx, nc, width * rows, LANES), f32),
-            pltpu.VMEM((slabs * crosses * rows, fringe), jnp.bfloat16),
-            pltpu.VMEM((LANES, fringe), f32),
-            pltpu.VMEM((width, fringe // LANES, LANES), f32),
-            pltpu.VMEM((tiles * MAT_ROWS, LANES), f32),
-            pltpu.VMEM((width * width, tiles, LANES), f32),
-            pltpu.VMEM((tiles * VEC_ROWS, LANES), f32),
-            pltpu.VMEM((slabs, MAT_ROWS, LANES), f32),
-            pltpu.VMEM((slabs, VEC_ROWS, LANES), f32),
-            pltpu.VMEM((slabs, VEC_ROWS, LANES), f32),
-            pltpu.VMEM((tiles * VEC_ROWS, LANES), f32),
-            dma((nz + ny + nx + nc,)),
-            dma((nz + ny + nx + nc,)),
-            dma((solvers,)),
-            dma((slabs,)),
-            dma((solvers,)),
-            dma((slabs,)),
-            dma((slabs,)),
-            dma((solvers,)),
-        ],
-        compiler_params=pltpu.CompilerParams(
-            collective_id=0, has_side_effects=True, vmem_limit_bytes=40 * 2**20
-        ),
-    )(
+    copies = (nz - 1) + 2 * (ny + nx + nc - 3)
+    operands = (
         by_tile(state),
         by_tile(rhs),
         by_tile(dinv),
@@ -426,6 +415,39 @@
         weights,
         receptor_perm,
     )
+    made = pl.pallas_call(
+        functools.partial(kernel, dims),
+        out_shape=jax.ShapeDtypeStruct((width * rows, LANES), f32),
+        in_specs=[pl.BlockSpec(memory_space=pltpu.HBM)] * 10,
+        out_specs=vmem,
+        scratch_shapes=[
+            *(pltpu.VMEM(a.shape, a.dtype) for a in operands[:-1]),
+            pltpu.SMEM(receptor_perm.shape, receptor_perm.dtype),
+            dma((len(operands),)),
+            pltpu.VMEM((nc, nz, ny, nx, width * rows, LANES), f32),
+            pltpu.VMEM((slabs * crosses * rows, fringe), jnp.bfloat16),
+            pltpu.VMEM((LANES, fringe), f32),
+            pltpu.VMEM((width, fringe // LANES, LANES), f32),
+            pltpu.VMEM((tiles * MAT_ROWS, LANES), f32),
+            pltpu.VMEM((width * width, tiles, LANES), f32),
+            pltpu.VMEM((tiles * VEC_ROWS, LANES), f32),
+            pltpu.VMEM((slabs, MAT_ROWS, LANES), f32),
+            pltpu.VMEM((slabs, VEC_ROWS, LANES), f32),
+            pltpu.VMEM((slabs, VEC_ROWS, LANES), f32),
+            pltpu.VMEM((tiles * VEC_ROWS, LANES), f32),
+            dma((copies,)),
+            dma((copies,)),
+            dma((solvers,)),
+            dma((slabs,)),
+            dma((solvers,)),
+            dma((slabs,)),
+            dma((slabs,)),
+            dma((solvers,)),
+        ],
+        compiler_params=pltpu.CompilerParams(
+            collective_id=0, has_side_effects=True, vmem_limit_bytes=62 * 2**20
+        ),
+    )(*operands)
     made = jnp.swapaxes(made.reshape(width, tiles, planes, LANES), 1, 2)
     return made.reshape(width, planes, cells)
 

time: 45.1 us -> 36.4 us (0.81)
  local copies, waits for them, and re-layouts: 7.18 us -> 1.4 us
  Pallas kernels: 37.4 us -> 34.9 us
    unnamed x21 -> x1, local copies, waits for them, and re-layouts: 7.18 us -> 1.4 us
    pallas_call x1, Pallas kernels: 37.4 us -> 34.9 us  [body(): pl.pallas_call(functools.partial(kernel, dims), out_shape=jax.ShapeDtypeS...]
where the time goes in v2:
time: 36.4 us; the launch traced here: 36.3 us
  Pallas kernels  34.9 us (96%)
  local copies, waits for them, and re-layouts  1.4 us (4%)
    pallas_call x1, Pallas kernels, body(): pl.pallas_call(functools.partial(kernel, dims), out_shape=jax.ShapeDtypeS...  34.9 us
    unnamed x1, local copies, waits for them, and re-layouts  1.4 us

profile of v2, /device:TPU:0, one launch (start us, length us, event | category | flops | bytes accessed | tf_op | source)
XLA Modules:
  0.0 36.3 jit_solution(1540015635675508336)
XLA Ops:
  0.0 34.9 %shard_map.100 = f32[80,128]{1,0:T(8,128)} custom-call(f32[80,128]{1,0:T(8,128)} %bitcast.36, f32[80,128]{1,0:T(8,128)} %bitcast.37, f32[400,128]{1,0:T(8,128)} %bitcast.32, f32[400,128]{1,0:T(8,128)} %bitcast.33, f32[400,128]{1,0:T(8,128)} %bitcast.34, s32[1,1024]{1,0:T(1,128)} %bitcast.38, s32[1,1024]{1,0:T(1,128)} %bitcast.39, s32[8,1024]{1,0:T(8,128)} %refs_7_.1, ...), custom_call_target="tpu_custom_call" | custom-call | tf_op jit(solution)/shard_map/pallas_call | solution.py:418
  34.9 1.4 %copy.18 = f32[5,2,1024]{2,1,0:T(2,128)} copy(f32[5,2,1024]{2,1,0:T(2,128)} %bitcast.35) | data formatting | bytes 81920

commit v3 on v2

--- a/solution.py
+++ b/solution.py
@@ -211,7 +211,6 @@
     first_x = pass_on(nx, x_peer, gath.at[w, :, :, x, first])
     finish(second_x)
     second_y = pass_on(ny, y_peer, gath.at[w, :, y, :, second])
-    scatter(lambda copy: copy.start(), mats, MAT_ROWS, mrecv, m_send, m_recv)
 
     blocks = donor[...]
     group = nz * ny * nx
@@ -230,6 +229,7 @@
     by_core = pass_on(nc, w_peer, gath.at[w, :, :, :, second])
     finish(first_x)
     by_core += pass_on(nc, w_peer, gath.at[w, :, :, :, first])
+    scatter(lambda copy: copy.start(), mats, MAT_ROWS, mrecv, m_send, m_recv)
 
     part = group * rows
 

time: 36.4 us -> 35.3 us (0.970)
  Pallas kernels: 34.9 us -> 33.7 us
    pallas_call x1, Pallas kernels: 34.9 us -> 33.7 us  [body(): pl.pallas_call(functools.partial(kernel, dims), out_shape=jax.ShapeDtypeS...]
where the time goes in v3:
time: 35.3 us; the launch traced here: 35.1 us
  Pallas kernels  33.7 us (95%)
  local copies, waits for them, and re-layouts  1.4 us (4%)
    pallas_call x1, Pallas kernels, body(): pl.pallas_call(functools.partial(kernel, dims), out_shape=jax.ShapeDtypeS...  33.7 us
    unnamed x1, local copies, waits for them, and re-layouts  1.4 us

profile of v3, /device:TPU:0, one launch (start us, length us, event | category | flops | bytes accessed | tf_op | source)
XLA Modules:
  0.0 35.1 jit_solution(2387679495625219884)
XLA Ops:
  0.0 33.7 %shard_map.100 = f32[80,128]{1,0:T(8,128)} custom-call(f32[80,128]{1,0:T(8,128)} %bitcast.36, f32[80,128]{1,0:T(8,128)} %bitcast.37, f32[400,128]{1,0:T(8,128)} %bitcast.32, f32[400,128]{1,0:T(8,128)} %bitcast.33, f32[400,128]{1,0:T(8,128)} %bitcast.34, s32[1,1024]{1,0:T(1,128)} %bitcast.38, s32[1,1024]{1,0:T(1,128)} %bitcast.39, s32[8,1024]{1,0:T(8,128)} %refs_7_.1, ...), custom_call_target="tpu_custom_call" | custom-call | tf_op jit(solution)/shard_map/pallas_call | solution.py:418
  33.7 1.4 %copy.18 = f32[5,2,1024]{2,1,0:T(2,128)} copy(f32[5,2,1024]{2,1,0:T(2,128)} %bitcast.35) | data formatting | bytes 81920
